TPU v7x, 32 devices: a whole 2x2x4 slice. The times are simulated.
32 devices in a mesh: row: 4 (over y, core), col: 8 (over z, x).
Axes of the slice: x: 2, y: 2, z: 4, core: 2. Of those that a mesh axis runs over, the one named last changes fastest.
Arguments:
- wavefunction: bfloat16 [4096, 4096], P('row', 'col'), may hold values from -6 to 6
- left_env: bfloat16 [4, 4096, 4096], P(None, 'row'), may hold values from -0.09375 to 0.09375
- right_env: bfloat16 [4, 4096, 4096], P(None, None, 'col'), may hold values from -0.09375 to 0.09375
- filled_blocks: int32 [32, 32], replicated, may hold values 0 or 1
- term_columns: int32 [4, 32], replicated, may hold values 0 or 1
Outputs:
- product: bfloat16 [4096, 4096], P('row', 'col')
All inputs are finite; a program needn't handle non-finite values.
Results may differ from a plain program's by a relative error of at most 0.001.
Values may be sent and summed in bfloat16 or wider, within the bound.
No kernel may reach another device: no remote copies, remote signals or barrier semaphores. Data moves between devices by JAX's collectives and lax.ppermute only.
A program may use at most 128 MiB of HBM per device.

v0:
```python
import jax
import jax.numpy as jnp
from jax import lax
from jax.sharding import PartitionSpec as P

BLOCK = 128


def on_device(wavefunction, left_env, right_env, filled_blocks, term_columns):
    row_count = wavefunction.shape[0]
    col_count = wavefunction.shape[1]
    row_blocks = row_count // BLOCK
    col_blocks = col_count // BLOCK
    row_place = lax.axis_index("row")
    col_place = lax.axis_index("col")
    filled_here = lax.dynamic_slice(
        filled_blocks, (row_place * row_blocks, col_place * col_blocks), (row_blocks, col_blocks)
    )
    block_gate = filled_here[:, None, :, None]
    masked_psi = (
        wavefunction.reshape(row_blocks, BLOCK, col_blocks, BLOCK) * block_gate.astype(jnp.bfloat16)
    ).reshape(row_count, col_count)
    column_gate = jnp.repeat(term_columns, BLOCK, axis=1).astype(jnp.bfloat16)
    acting = left_env * column_gate[:, None, :]
    window = right_env
    right_terms = jnp.einsum(
        "kc,tcb->tkb",
        lax.all_gather(masked_psi, "col", axis=1, tiled=True),
        window,
        preferred_element_type=jnp.float32,
    )
    window = acting.astype(jnp.float32)
    summed = jnp.einsum(
        "tak,tkb->ab",
        window,
        lax.all_gather(right_terms, "row", axis=1, tiled=True),
        precision=lax.Precision.HIGHEST,
        preferred_element_type=jnp.float32,
    )
    result = summed.reshape(row_blocks, BLOCK, col_blocks, BLOCK) * block_gate.astype(jnp.float32)
    return result.reshape(row_count, col_count).astype(jnp.bfloat16)


def solution(mesh):
    in_specs = (P("row", "col"), P(None, "row", None), P(None, None, "col"), P(), P())
    out_specs = P("row", "col")
    return jax.shard_map(
        on_device, mesh=mesh, in_specs=in_specs, out_specs=out_specs, check_vma=False
    )
```

profile of v0, /device:TPU:0, one launch (start us, length us, event | category | flops | bytes accessed | tf_op | source)
XLA Modules:
  0.0 428.1 jit_solution(2758140171862974396)
XLA Ops:
  6.5 0.0 all-gather.3.cloned.1.call-start
  6.5 0.8 dynamic-slice_convert_fusion.1
  7.3 0.3 mul.40
  7.6 2.3 bitcast_multiply_fusion.1
  10.0 0.0 all-gather.3.cloned.1.call-update
  10.0 0.0 copy-start
  10.0 0.0 all-gather.5.cloned.1.call-start
  10.1 128.2 %all-gather.3.cloned.1.call-done = bf16[1024,4096]{1,0:T(8,128)(2,1)} async-done(((bf16[1024,512]{1,0:T(8,128)(2,1)}), bf16[1024,4096]{1,0:T(8,128)(2,1)}) %all-gather.3.cloned.1.call-update) | async-done | bytes 8388624 | tf_op jit(solution)/shard_map/all_gather | solution.py:28
  138.2 24.0 %fusion.5 = f32[4,1024,512]{2,1,0:T(8,128)} fusion(bf16[4,4096,512]{2,1,0:T(8,128)(2,1)} %param.7, bf16[1024,4096]{1,0:T(8,128)(2,1)} %all-gather.3.cloned.1.call-done), kind=kOutput, calls=%fused_computation.5 | convolution fusion | flops 17179869184 | bytes 33554432 | tf_op jit(solution)/shard_map/kc,tcb->tkb/dot_general | solution.py:26
  162.3 0.0 all-gather.5.cloned.1.call-update
  162.3 0.0 copy-done
  162.3 0.1 broadcast_bitcast_fusion
  162.4 199.7 %all-gather.5.cloned.1.call-done = f32[4,4096,512]{2,1,0:T(8,128)} async-done(((f32[4,1024,512]{2,1,0:T(8,128)}), f32[4,4096,512]{2,1,0:T(8,128)}) %all-gather.5.cloned.1.call-update) | async-done | bytes 33554448 | tf_op jit(solution)/shard_map/all_gather | solution.py:36
  362.2 0.3 mul.43
  362.5 58.8 %fusion.8 = bf16[1024,512]{1,0:T(8,128)(2,1)} fusion(f32[128,8,4,128]{3,2,1,0:T(4,128)S(1)} %bitcast.30, f32[4,4096,512]{2,1,0:T(8,128)} %all-gather.5.cloned.1.call-done, bf16[4,1024,4096]{2,1,0:T(8,128)(2,1)} %param.6, bf16[4,4096]{1,0:T(4,128)(2,1)S(1)} %bitcast.31), kind=kOutput, calls=%fused_computation.7 | convolution fusion | flops 103097040896 | bytes 70287360 | tf_op jit(solution)/shard_map/tak,tkb->ab/dot_general | solution.py:33
  (2 shorter events, 0.0 us)
Async XLA Ops:
  6.5 131.7 %all-gather.3.cloned.1.call-start = ((), (), s32[]{:S(2)}) async-start(), calls=%async_computation | async-start | bytes 9437184 | tf_op jit(solution)/shard_map/all_gather | solution.py:28
  10.0 152.3 %copy-start = (s32[4,32]{1,0:T(4,128)S(1)}, s32[4,32]{1,0:T(4,128)}, u32[]{:S(2)}) copy-start(s32[4,32]{1,0:T(4,128)} %param.9) | copy-start | bytes 1540
  10.0 352.1 %all-gather.5.cloned.1.call-start = ((), (), s32[]{:S(2)}) async-start(), calls=%async_computation.1 | async-start | bytes 41943040 | tf_op jit(solution)/shard_map/all_gather | solution.py:36
Sparse Core Ops, SparseCore 0:
  10.1 128.0 all-gather.2
  162.4 199.7 all-gather.4
where the time goes:
time: 428 us
  waiting for transfers between devices  328 us (77%)
  matrix products  82.8 us (19%)
  between operations  13.5 us (3%)
    all_gather x1, waiting for transfers between devices, on_device(): lax.all_gather(right_terms, 'row', axis=1, tiled=True)  200 us
    all_gather x1, waiting for transfers between devices, on_device(): lax.all_gather(masked_psi, 'col', axis=1, tiled=True)  128 us
    dot_general x1, matrix products, on_device(): jnp.einsum('tak,tkb->ab', window, lax.all_gather(right_terms, 'row', axis...  58.8 us
    dot_general x1, matrix products, on_device(): jnp.einsum('kc,tcb->tkb', lax.all_gather(masked_psi, 'col', axis=1, tiled...  24 us
  transfers between devices with their start and end apart: 2, of which 2 were waited for; matrix products, arithmetic and copies ran while one was open for 0% of the time, Pallas kernels for 0%

commit v1 on v0

v1 whole, which is shorter than its diff:
```python
import functools

import jax
import jax.numpy as jnp
from jax import lax
from jax.experimental import pallas as pl
from jax.experimental.pallas import tpu as pltpu
from jax.sharding import PartitionSpec as P

BLOCK = 128
CORES = 2
GROUP = 4
CHUNK = 4
AXES = ("row", "col")
VMEM_LIMIT = 58 * 1024 * 1024


class Places:
    def __init__(self, row_devices, col_devices):
        self.rows, self.cols = row_devices, col_devices
        self.y = row_devices // CORES
        self.x = 1
        while self.x * self.x * 4 <= col_devices and col_devices % (self.x * 2) == 0:
            self.x *= 2
        self.z = col_devices // self.x

    def flat(self, y, core, z, x):
        return (y * CORES + core) * self.cols + z * self.x + x

    def shift(self, dy=0, dz=0, dx=0, dcore=0):
        perm = []
        for y in range(self.y):
            for core in range(CORES):
                for z in range(self.z):
                    for x in range(self.x):
                        there = self.flat(
                            (y + dy) % self.y, (core + dcore) % CORES, (z + dz) % self.z, (x + dx) % self.x
                        )
                        perm.append((self.flat(y, core, z, x), there))
        return perm


def compress_kernel(ranges, row_blocks, col_blocks, filled, psi, *rest):
    outs, sems = rest[: len(ranges)], rest[len(ranges)]
    row0 = lax.axis_index("row") * row_blocks
    col0 = lax.axis_index("col") * col_blocks

    def copy(out, low, spot, kb, cb):
        return pltpu.make_async_copy(
            psi.at[pl.ds(kb * BLOCK, BLOCK), pl.ds(cb * BLOCK, BLOCK)], out.at[spot - low], sems.at[spot]
        )

    count = jnp.int32(0)
    for kb in range(row_blocks):
        for cb in range(col_blocks):
            here = filled[row0 + kb, col0 + cb]
            for out, (low, high) in zip(outs, ranges):
                @pl.when((here != 0) & (count >= low) & (count < high))
                def _():
                    copy(out, low, count, kb, cb).start()
            count = count + here
    for out, (low, high) in zip(outs, ranges):
        for spot in range(low, high):
            @pl.when(spot < count)
            def _():
                copy(out, low, spot, 0, 0).wait()


def compress(psi, filled, ranges):
    row_blocks, col_blocks = psi.shape[0] // BLOCK, psi.shape[1] // BLOCK
    return pl.pallas_call(
        functools.partial(compress_kernel, ranges, row_blocks, col_blocks),
        out_shape=[jax.ShapeDtypeStruct((high - low, BLOCK, BLOCK), psi.dtype) for low, high in ranges],
        in_specs=[pl.BlockSpec(memory_space=pltpu.SMEM), pl.BlockSpec(memory_space=pl.ANY)],
        out_specs=[pl.BlockSpec(memory_space=pl.ANY)] * len(ranges),
        scratch_shapes=[pltpu.SemaphoreType.DMA((row_blocks * col_blocks,))],
        name="compress",
    )(filled, psi)


class Layout:
    def __init__(self, places, row_blocks, col_blocks, terms, base):
        self.places, self.row_blocks, self.col_blocks, self.terms, self.base = places, row_blocks, col_blocks, terms, base
        self.slots = row_blocks * col_blocks
        self.states = places.y * row_blocks
        self.old_right = places.cols * col_blocks
        self.shards = places.y * places.z * places.x
        self.stride = self.old_right + CHUNK
        self.pairs = self.states * terms + GROUP
        self.tile = 2 if col_blocks % 2 == 0 else 1
        self.tiles = col_blocks // self.tile
        self.new_left = CORES * row_blocks
        self.trash = self.new_left
        self.list_stride = self.new_left + 2

    def shapes(self):
        return [
            ((self.states + 1) * 1,),
            (self.states * self.stride,),
            (self.states * self.stride,),
            (self.pairs,),
            (self.pairs,),
            (self.tiles * self.list_stride,),
            (1 + self.tiles,),
        ]


def plan_kernel(lay, filled, terms, counts, spots, blocks, pair_q, pair_t, lefts, totals, used, base_of):
    pz, px, py = lay.places.z, lay.places.x, lay.places.y
    row, col = lax.axis_index("row"), lax.axis_index("col")
    core, y_me = row % CORES, row // CORES
    z_me, x_me = col // px, col % px
    for dev in range(lay.places.cols):
        dz = (z_me - dev // px + pz) % pz
        dx = (x_me - dev % px + px) % px
        base_of[dev] = dz * px + dx

    extra = lay.slots - lay.base

    def one_state(q, n_pairs):
        y = q // lay.row_blocks
        kb = q % lay.row_blocks

        @pl.when(kb == 0)
        def _():
            for dev in range(lay.places.cols):
                used[dev] = 0

        dy = (y_me - y + py) % py
        k_block = (y * CORES + core) * lay.row_blocks + kb
        n = jnp.int32(0)
        for c in range(lay.old_right):
            dev = c // lay.col_blocks
            here = filled[k_block, c]
            slot = used[dev]
            shard = dy * (pz * px) + base_of[dev]
            spot = jnp.where(
                slot < lay.base,
                1 + shard * lay.base + slot,
                1 + lay.shards * lay.base + shard * extra + slot - lay.base,
            )
            spots[q * lay.stride + n] = spot
            blocks[q * lay.stride + n] = c
            n = n + here
            used[dev] = slot + here
        for i in range(CHUNK):
            spots[q * lay.stride + n + i] = 0
            blocks[q * lay.stride + n + i] = 0
        counts[q] = n
        for t in range(lay.terms):
            pair_q[n_pairs] = q
            pair_t[n_pairs] = t
            n_pairs = n_pairs + jnp.where((terms[t, k_block] != 0) & (n > 0), 1, 0)
        return n_pairs

    n_pairs = lax.fori_loop(0, lay.states, one_state, jnp.int32(0))
    counts[lay.states] = 0
    for i in range(GROUP):
        pair_q[n_pairs + i] = lay.states
        pair_t[n_pairs + i] = 0
    totals[0] = (n_pairs + GROUP - 1) // GROUP
    for tile in range(lay.tiles):
        n = jnp.int32(0)
        for a in range(lay.new_left):
            side, ab = a // lay.row_blocks, a % lay.row_blocks
            a_block = (y_me * CORES + (core + side) % CORES) * lay.row_blocks + ab
            some = jnp.int32(0)
            for i in range(lay.tile):
                some = some | filled[a_block, col * lay.col_blocks + tile * lay.tile + i]
            lefts[tile * lay.list_stride + n] = a
            n = n + some
        lefts[tile * lay.list_stride + n] = lay.trash
        totals[1 + tile] = (n + 1) // 2


def plan(lay, filled, terms):
    smem = pl.BlockSpec(memory_space=pltpu.SMEM)
    shapes = lay.shapes()
    return pl.pallas_call(
        functools.partial(plan_kernel, lay),
        out_shape=[jax.ShapeDtypeStruct(s, jnp.int32) for s in shapes],
        in_specs=[smem, smem],
        out_specs=[smem] * len(shapes),
        scratch_shapes=[pltpu.SMEM((lay.places.cols,), jnp.int32), pltpu.SMEM((lay.places.cols,), jnp.int32)],
        name="plan",
    )(filled, terms)


def main_kernel(lay, widths, rows, n_sib, *refs):
    refs = list(refs)
    counts, spots, blocks, pair_q, pair_t, lefts, totals = refs[:7]
    right, left = refs[7], refs[8]
    sib = refs[9 : 9 + n_sib]
    n_psi = len(widths) * lay.shards
    psi_in = refs[9 + n_sib : 9 + n_sib + n_psi]
    out_own, out_sib = refs[9 + n_sib + n_psi : 11 + n_sib + n_psi]
    (right_v, psi_v, left_v, acc, w_hi, w_lo, w_acc, right_sem, psi_sem, left_sem, out_sem) = refs[11 + n_sib + n_psi :]
    core = lax.axis_index("row") % CORES
    terms = lay.terms

    def left_copies(g, slot, act):
        for i in range(GROUP):
            q = jnp.minimum(pair_q[g * GROUP + i], lay.states - 1)
            t = pair_t[g * GROUP + i]
            y, kb = q // lay.row_blocks, q % lay.row_blocks
            at = pl.multiple_of(((y * CORES + core) * lay.row_blocks + kb) * BLOCK, BLOCK)
            lanes = pl.ds(i * BLOCK, BLOCK)
            act(
                pltpu.make_async_copy(
                    left.at[t, :, pl.ds(at, BLOCK)], left_v.at[slot, pl.ds(0, rows), lanes], left_sem.at[slot, 2 * i]
                )
            )
            there = pl.multiple_of(kb * BLOCK, BLOCK)
            for yy in range(n_sib):
                @pl.when(y == yy)
                def _():
                    act(
                        pltpu.make_async_copy(
                            sib[yy].at[t, :, pl.ds(there, BLOCK)],
                            left_v.at[slot, pl.ds(rows, rows), lanes],
                            left_sem.at[slot, 2 * i + 1],
                        )
                    )

    loads = []
    for t in range(terms):
        loads.append(pltpu.make_async_copy(right.at[t], right_v.at[t], right_sem.at[t]))
    for part in range(len(widths)):
        for s in range(lay.shards):
            i = part * lay.shards + s
            loads.append(psi_load(lay, widths, part, s, psi_in[i], psi_v, psi_sem.at[i]))
    for load in loads:
        load.start()
    n_groups = totals[0]

    @pl.when(n_groups > 0)
    def _():
        left_copies(0, 0, lambda c: c.start())

    psi_v[0] = jnp.zeros((BLOCK, BLOCK), psi_v.dtype)
    acc[...] = jnp.zeros_like(acc)
    for load in loads:
        load.wait()

    def one_group(g, carry):
        slot = g % 2

        @pl.when(g + 1 < n_groups)
        def _():
            left_copies(g + 1, 1 - slot, lambda c: c.start())

        def one_pair(i, c0):
            q = pair_q[g * GROUP + i]
            t = pair_t[g * GROUP + i]
            w_acc[...] = jnp.zeros_like(w_acc)

            def one_chunk(j, c1):
                at = q * lay.stride + j * CHUNK
                lhs = jnp.concatenate([psi_v[spots[at + m]] for m in range(CHUNK)], axis=1)
                rhs = jnp.concatenate(
                    [
                        right_v[t, pl.ds(pl.multiple_of(blocks[at + m] * BLOCK, BLOCK), BLOCK), :]
                        for m in range(CHUNK)
                    ],
                    axis=0,
                )
                w_acc[...] += jnp.dot(lhs, rhs, preferred_element_type=jnp.float32)
                return c1

            lax.fori_loop(0, (counts[q] + CHUNK - 1) // CHUNK, one_chunk, 0)
            whole = w_acc[...]
            hi = whole.astype(jnp.bfloat16)
            at = pl.ds(pl.multiple_of(i * BLOCK, BLOCK), BLOCK)
            w_hi[at, :] = hi
            w_lo[at, :] = (whole - hi.astype(jnp.float32)).astype(jnp.bfloat16)
            return c0

        lax.fori_loop(0, GROUP, one_pair, 0)
        left_copies(g, slot, lambda c: c.wait())
        for tile in range(lay.tiles):
            width = lay.tile * BLOCK
            lanes = slice(tile * width, (tile + 1) * width)

            def two_lefts(m, c0):
                a0 = lefts[tile * lay.list_stride + 2 * m]
                a1 = lefts[tile * lay.list_stride + 2 * m + 1]
                from1 = jnp.minimum(a1, lay.new_left - 1)
                at0 = pl.ds(pl.multiple_of(a0 * BLOCK, BLOCK), BLOCK)
                at1 = pl.ds(pl.multiple_of(a1 * BLOCK, BLOCK), BLOCK)
                lhs = jnp.concatenate(
                    [left_v[slot, at0, :], left_v[slot, pl.ds(pl.multiple_of(from1 * BLOCK, BLOCK), BLOCK), :]], axis=0
                )
                gain = jnp.dot(lhs, w_hi[:, lanes], preferred_element_type=jnp.float32)
                gain = gain + jnp.dot(lhs, w_lo[:, lanes], preferred_element_type=jnp.float32)
                acc[at0, lanes] += gain[:BLOCK]
                acc[at1, lanes] += gain[BLOCK:]
                return c0

            lax.fori_loop(0, totals[1 + tile], two_lefts, 0)
        return carry

    lax.fori_loop(0, n_groups, one_group, 0)
    stores = [
        pltpu.make_async_copy(acc.at[pl.ds(rows, rows)], out_sib, out_sem.at[1]),
        pltpu.make_async_copy(acc.at[pl.ds(0, rows)], out_own, out_sem.at[0]),
    ]
    for store in stores:
        store.start()
    for store in stores:
        store.wait()


def psi_load(lay, widths, part, s, source, psi_v, sem):
    if part < 2:
        low = 1 + s * lay.base + sum(widths[:part])
    else:
        low = 1 + lay.shards * lay.base + s * (lay.slots - lay.base) + sum(widths[2:part])
    return pltpu.make_async_copy(source, psi_v.at[pl.ds(low, widths[part])], sem)


def contract(lay, tables, right, left, sib, parts):
    rows = lay.row_blocks * BLOCK
    cols = lay.col_blocks * BLOCK
    widths = [part[0].shape[0] for part in parts]
    flat = [array for part in parts for array in part]
    smem = pl.BlockSpec(memory_space=pltpu.SMEM)
    hbm = pl.BlockSpec(memory_space=pl.ANY)
    result = jax.ShapeDtypeStruct((rows, cols), jnp.float32)
    return pl.pallas_call(
        functools.partial(main_kernel, lay, widths, rows, len(sib)),
        out_shape=[result, result],
        in_specs=[smem] * len(tables) + [hbm] * (2 + len(sib) + len(flat)),
        out_specs=[hbm, hbm],
        scratch_shapes=[
            pltpu.VMEM(right.shape, jnp.bfloat16),
            pltpu.VMEM((1 + lay.shards * sum(widths), BLOCK, BLOCK), jnp.bfloat16),
            pltpu.VMEM((2, CORES * rows, GROUP * BLOCK), jnp.bfloat16),
            pltpu.VMEM((CORES * rows + BLOCK, cols), jnp.float32),
            pltpu.VMEM((GROUP * BLOCK, cols), jnp.bfloat16),
            pltpu.VMEM((GROUP * BLOCK, cols), jnp.bfloat16),
            pltpu.VMEM((BLOCK, cols), jnp.float32),
            pltpu.SemaphoreType.DMA((lay.terms,)),
            pltpu.SemaphoreType.DMA((len(flat),)),
            pltpu.SemaphoreType.DMA((2, 2 * GROUP)),
            pltpu.SemaphoreType.DMA((2,)),
        ],
        compiler_params=pltpu.CompilerParams(vmem_limit_bytes=VMEM_LIMIT),
        name="contract",
    )(*tables, right, left, *sib, *flat)


def spread(places, part, x_first):
    got = {(0, 0, 0): part}
    for dz in range(1, places.z):
        got[(0, dz, 0)] = lax.ppermute(part, AXES, places.shift(dz=dz))
    for axis in ("xy" if x_first else "yx"):
        have = dict(got)
        for (dy, dz, dx), array in have.items():
            if axis == "x":
                for step in range(1, places.x):
                    got[(dy, dz, step)] = lax.ppermute(array, AXES, places.shift(dx=step))
            else:
                for step in range(1, places.y):
                    got[(step, dz, dx)] = lax.ppermute(array, AXES, places.shift(dy=step))
    order = [(dy, dz, dx) for dy in range(places.y) for dz in range(places.z) for dx in range(places.x)]
    return [got[key] for key in order]


def on_device(wavefunction, left_env, right_env, filled_blocks, term_columns):
    rows, cols = wavefunction.shape
    row_blocks, col_blocks = rows // BLOCK, cols // BLOCK
    places = Places(lax.axis_size("row"), lax.axis_size("col"))
    slots = row_blocks * col_blocks
    base = -(-slots * 9 // 32) * 2
    extra = slots - base
    lay = Layout(places, row_blocks, col_blocks, left_env.shape[0], base)
    row_place, col_place = lax.axis_index("row"), lax.axis_index("col")

    cuts = [0, base // 2, base, base + extra // 2, slots]
    ranges = [(low, high) for low, high in zip(cuts[:-1], cuts[1:]) if high > low]
    packed = list(compress(wavefunction, filled_blocks, ranges))

    other = (row_place + 1) % CORES
    packed[0], left_late = lax.optimization_barrier((packed[0], left_env))
    parts = [spread(places, packed[0], True), spread(places, packed[1], False)]
    swap = places.shift(dcore=1)
    sib = [
        lax.ppermute(
            lax.dynamic_slice(left_late, (0, 0, (y * CORES + other) * rows), (left_env.shape[0], rows, rows)), AXES, swap
        )
        for y in range(places.y)
    ]
    tables = plan(lay, filled_blocks, term_columns)

    per_device = filled_blocks.reshape(places.rows, row_blocks, places.cols, col_blocks).sum(axis=(1, 3))

    def more(_):
        rest = [spread(places, part, i == 0) for i, part in enumerate(packed[2:])]
        return contract(lay, tables, right_env, left_env, sib, parts + rest)

    def enough(_):
        return contract(lay, tables, right_env, left_env, sib, parts)

    own, theirs = lax.cond(jnp.max(per_device) > base, more, enough, 0)
    summed = own + lax.ppermute(theirs, AXES, swap)
    here = lax.dynamic_slice(
        filled_blocks, (row_place * row_blocks, col_place * col_blocks), (row_blocks, col_blocks)
    )
    result = jnp.where(
        here[:, None, :, None] != 0, summed.reshape(row_blocks, BLOCK, col_blocks, BLOCK), jnp.float32(0)
    )
    return result.reshape(rows, cols).astype(jnp.bfloat16)


def solution(mesh):
    in_specs = (P("row", "col"), P(None, "row", None), P(None, None, "col"), P(), P())
    out_specs = P("row", "col")
    return jax.shard_map(
        on_device, mesh=mesh, in_specs=in_specs, out_specs=out_specs, check_vma=False
    )
```

time: 428 us -> 283 us (0.66)
  waiting for transfers between devices: 328 us -> 84.3 us
  Pallas kernels: 0 us -> 115 us
  matrix products: 82.8 us -> 0 us
  starting transfers between devices: 0.04 us -> 61.1 us
  local copies, waits for them, and re-layouts: 0.78 us -> 15 us
  between operations: 13.5 us -> 0.89 us
    all_gather x2 -> x0, waiting for transfers between devices: 328 us -> none  [the longest x1 200 us: on_device(): lax.all_gather(right_terms, 'row', axis=1, tiled=True)]
    pallas_call x0 -> x3, Pallas kernels: none -> 115 us  [the longest x1 108 us: contract(): pl.pallas_call(functools.partial(main_kernel, lay, widths, rows, len(sib)...]
    ppermute x0 -> x33, waiting for transfers between devices: none -> 84.3 us  [the longest x12 39.8 us: spread(): got[step, dz, dx] = lax.ppermute(array, AXES, places.shift(dy=step))]
    dot_general x2 -> x0, matrix products: 82.8 us -> none  [the longest x1 58.8 us: on_device(): jnp.einsum('tak,tkb->ab', window, lax.all_gather(right_terms, 'row', axis...]
    ppermute x0 -> x33, starting transfers between devices: none -> 61.1 us  [the longest x6 35.9 us: spread(): got[0, dz, 0] = lax.ppermute(part, AXES, places.shift(dz=dz))]
    dynamic_slice x0 -> x1, local copies, waits for them, and re-layouts: none -> 11.8 us  [on_device(): lax.dynamic_slice(left_late, (0, 0, (y * CORES + other) * rows), (left_en...]
  transfers between devices with their start and end apart: 2 -> 33, of which waited for: 2 -> 22; matrix products, arithmetic and copies ran while one was open for 0% -> 2% of each run, Pallas kernels for 0% -> 2%
where the time goes in v1:
time: 283 us; the launch traced here: 282 us
  Pallas kernels  115 us (41%)
  waiting for transfers between devices  84.3 us (30%)
  starting transfers between devices  61.1 us (22%)
  local copies, waits for them, and re-layouts  15 us (5%)
  other arithmetic  5.8 us (2%)
    pallas_call x1, Pallas kernels, contract(): pl.pallas_call(functools.partial(main_kernel, lay, widths, rows, len(sib)...  108 us
    ppermute x12, waiting for transfers between devices, spread(): got[step, dz, dx] = lax.ppermute(array, AXES, places.shift(dy=step))  39.8 us
    ppermute x6, starting transfers between devices, spread(): got[0, dz, 0] = lax.ppermute(part, AXES, places.shift(dz=dz))  35.9 us
    ppermute x12, waiting for transfers between devices, spread(): got[dy, dz, step] = lax.ppermute(array, AXES, places.shift(dx=step))  26.6 us
    ppermute x12, starting transfers between devices, spread(): got[dy, dz, step] = lax.ppermute(array, AXES, places.shift(dx=step))  16.3 us
    ppermute x6, waiting for transfers between devices, spread(): got[0, dz, 0] = lax.ppermute(part, AXES, places.shift(dz=dz))  14.3 us
    dynamic_slice x1, local copies, waits for them, and re-layouts, on_device(): lax.dynamic_slice(left_late, (0, 0, (y * CORES + other) * rows), (left_en...  11.8 us
    ppermute x12, starting transfers between devices, spread(): got[step, dz, dx] = lax.ppermute(array, AXES, places.shift(dy=step))  8.24 us
  transfers between devices with their start and end apart: 33, of which 22 were waited for; matrix products, arithmetic and copies ran while one was open for 2% of the time, Pallas kernels for 2%

profile of v1, /device:TPU:0, one launch (start us, length us, event | category | flops | bytes accessed | tf_op | source)
XLA Modules:
  0.0 282.4 jit_solution(11115656293387659805)
XLA Ops:
  0.0 2.6 compress.1
  2.6 11.8 %constant_dynamic-slice_fusion = (bf16[4,1024,1024]{2,1,0:T(8,128)(2,1)}, bf16[4,1024,1024]{2,1,0:T(8,128)(2,1)}) fusion(bf16[4,1024,4096]{2,1,0:T(8,128)(2,1)} %param.8, s32[]{:T(128)S(6)} %select_n.28, s32[]{:T(128)S(6)} %select_n.27), kind=kLoop, calls=%fused_computation.2 | loop fusion | bytes 33554440 | tf_op jit(solution)/shard_map/dynamic_slice | solution.py:389
  15.0 3.0 %collective-permute-start.33 = (bf16[9,128,128]{2,1,0:T(8,128)(2,1)S(1)}, bf16[9,128,128]{2,1,0:T(8,128)(2,1)S(1)}, u32[]{:S(2)}, u32[]{:S(2)}) collective-permute-start(bf16[9,128,128]{2,1,0:T(8,128)(2,1)S(1)} %get-tuple-element.293), channel_id=1, source_target_pairs={{0,2},{1,3},{2,4},{3,5},{4,6},{5,7},{6,0},{7,1},{8,10},{9,11},{10,... | collective-permute-start | bytes 884744 | tf_op jit(solution)/shard_map/ppermute | solution.py:355
  18.0 2.5 collective-permute-start.35
  21.9 6.0 %collective-permute-done.33 = bf16[9,128,128]{2,1,0:T(8,128)(2,1)S(1)} collective-permute-done((bf16[9,128,128]{2,1,0:T(8,128)(2,1)S(1)}, bf16[9,128,128]{2,1,0:T(8,128)(2,1)S(1)}, u32[]{:S(2)}, u32[]{:S(2)}) %collective-permute-start.33) | collective-permute-done | bytes 294944 | tf_op jit(solution)/shard_map/ppermute | solution.py:355
  27.9 11.3 %collective-permute-start.48 = (bf16[9,128,128]{2,1,0:T(8,128)(2,1)S(1)}, bf16[9,128,128]{2,1,0:T(8,128)(2,1)S(1)}, u32[]{:S(2)}, u32[]{:S(2)}) collective-permute-start(bf16[9,128,128]{2,1,0:T(8,128)(2,1)S(1)} %get-tuple-element.294), channel_id=1, source_target_pairs={{0,2},{1,3},{2,4},{3,5},{4,6},{5,7},{6,0},{7,1},{8,10},{9,11},{10,... | collective-permute-start | bytes 884744 | tf_op jit(solution)/shard_map/ppermute | solution.py:355
  41.5 16.7 %collective-permute-start.52 = (bf16[9,128,128]{2,1,0:T(8,128)(2,1)S(1)}, bf16[9,128,128]{2,1,0:T(8,128)(2,1)S(1)}, u32[]{:S(2)}, u32[]{:S(2)}) collective-permute-start(bf16[9,128,128]{2,1,0:T(8,128)(2,1)S(1)} %get-tuple-element.294), channel_id=1, source_target_pairs={{0,6},{1,7},{2,0},{3,1},{4,2},{5,3},{6,4},{7,5},{8,14},{9,15},{10,... | collective-permute-start | bytes 884744 | tf_op jit(solution)/shard_map/ppermute | solution.py:355
  59.7 5.5 %collective-permute-done.50 = bf16[9,128,128]{2,1,0:T(8,128)(2,1)S(1)} collective-permute-done((bf16[9,128,128]{2,1,0:T(8,128)(2,1)S(1)}, bf16[9,128,128]{2,1,0:T(8,128)(2,1)S(1)}, u32[]{:S(2)}, u32[]{:S(2)}) %collective-permute-start.50) | collective-permute-done | bytes 294944 | tf_op jit(solution)/shard_map/ppermute | solution.py:355
  65.3 1.6 collective-permute-start.54
  68.3 1.6 collective-permute-start.39
  71.3 3.8 %collective-permute-done.54 = bf16[9,128,128]{2,1,0:T(8,128)(2,1)S(1)} collective-permute-done((bf16[9,128,128]{2,1,0:T(8,128)(2,1)S(1)}, bf16[9,128,128]{2,1,0:T(8,128)(2,1)S(1)}, u32[]{:S(2)}, u32[]{:S(2)}) %collective-permute-start.54) | collective-permute-done | bytes 294944 | tf_op jit(solution)/shard_map/ppermute | solution.py:364
  75.2 1.6 collective-permute-start.34
  76.7 3.7 %collective-permute-done.39 = bf16[9,128,128]{2,1,0:T(8,128)(2,1)S(1)} collective-permute-done((bf16[9,128,128]{2,1,0:T(8,128)(2,1)S(1)}, bf16[9,128,128]{2,1,0:T(8,128)(2,1)S(1)}, u32[]{:S(2)}, u32[]{:S(2)}) %collective-permute-start.39) | collective-permute-done | bytes 294944 | tf_op jit(solution)/shard_map/ppermute | solution.py:364
  80.4 1.6 collective-permute-start.36
  82.5 3.7 %collective-permute-done.34 = bf16[9,128,128]{2,1,0:T(8,128)(2,1)} collective-permute-done((bf16[9,128,128]{2,1,0:T(8,128)(2,1)S(1)}, bf16[9,128,128]{2,1,0:T(8,128)(2,1)}, u32[]{:S(2)}, u32[]{:S(2)}) %collective-permute-start.34) | collective-permute-done | bytes 294944 | tf_op jit(solution)/shard_map/ppermute | solution.py:361
  86.4 6.0 %collective-permute-done.36 = bf16[9,128,128]{2,1,0:T(8,128)(2,1)S(1)} collective-permute-done((bf16[9,128,128]{2,1,0:T(8,128)(2,1)S(1)}, bf16[9,128,128]{2,1,0:T(8,128)(2,1)S(1)}, u32[]{:S(2)}, u32[]{:S(2)}) %collective-permute-start.36) | collective-permute-done | bytes 294944 | tf_op jit(solution)/shard_map/ppermute | solution.py:361
  92.6 4.6 %collective-permute-done.38 = bf16[9,128,128]{2,1,0:T(8,128)(2,1)S(1)} collective-permute-done((bf16[9,128,128]{2,1,0:T(8,128)(2,1)S(1)}, bf16[9,128,128]{2,1,0:T(8,128)(2,1)S(1)}, u32[]{:S(2)}, u32[]{:S(2)}) %collective-permute-start.38) | collective-permute-done | bytes 294944 | tf_op jit(solution)/shard_map/ppermute | solution.py:361
  97.7 1.6 collective-permute-start.41
  100.0 7.2 %collective-permute-done.60 = bf16[9,128,128]{2,1,0:T(8,128)(2,1)} collective-permute-done((bf16[9,128,128]{2,1,0:T(8,128)(2,1)S(1)}, bf16[9,128,128]{2,1,0:T(8,128)(2,1)}, u32[]{:S(2)}, u32[]{:S(2)}) %collective-permute-start.60) | collective-permute-done | bytes 294944 | tf_op jit(solution)/shard_map/ppermute | solution.py:364
  107.7 5.7 %collective-permute-done.41 = bf16[9,128,128]{2,1,0:T(8,128)(2,1)S(1)} collective-permute-done((bf16[9,128,128]{2,1,0:T(8,128)(2,1)S(1)}, bf16[9,128,128]{2,1,0:T(8,128)(2,1)S(1)}, u32[]{:S(2)}, u32[]{:S(2)}) %collective-permute-start.41) | collective-permute-done | bytes 294944 | tf_op jit(solution)/shard_map/ppermute | solution.py:364
  114.0 5.8 %collective-permute-done.43 = bf16[9,128,128]{2,1,0:T(8,128)(2,1)S(1)} collective-permute-done((bf16[9,128,128]{2,1,0:T(8,128)(2,1)S(1)}, bf16[9,128,128]{2,1,0:T(8,128)(2,1)S(1)}, u32[]{:S(2)}, u32[]{:S(2)}) %collective-permute-start.43) | collective-permute-done | bytes 294944 | tf_op jit(solution)/shard_map/ppermute | solution.py:364
  121.3 4.8 %collective-permute-done.45 = bf16[9,128,128]{2,1,0:T(8,128)(2,1)S(1)} collective-permute-done((bf16[9,128,128]{2,1,0:T(8,128)(2,1)S(1)}, bf16[9,128,128]{2,1,0:T(8,128)(2,1)S(1)}, u32[]{:S(2)}, u32[]{:S(2)}) %collective-permute-start.45) | collective-permute-done | bytes 294944 | tf_op jit(solution)/shard_map/ppermute | solution.py:364
  127.7 3.1 %collective-permute-done.40 = bf16[9,128,128]{2,1,0:T(8,128)(2,1)S(1)} collective-permute-done((bf16[9,128,128]{2,1,0:T(8,128)(2,1)S(1)}, bf16[9,128,128]{2,1,0:T(8,128)(2,1)S(1)}, u32[]{:S(2)}, u32[]{:S(2)}) %collective-permute-start.40) | collective-permute-done | bytes 294944 | tf_op jit(solution)/shard_map/ppermute | solution.py:364
  134.7 6.0 %collective-permute-done.53 = bf16[9,128,128]{2,1,0:T(8,128)(2,1)S(1)} collective-permute-done((bf16[9,128,128]{2,1,0:T(8,128)(2,1)S(1)}, bf16[9,128,128]{2,1,0:T(8,128)(2,1)S(1)}, u32[]{:S(2)}, u32[]{:S(2)}) %collective-permute-start.53) | collective-permute-done | bytes 294944 | tf_op jit(solution)/shard_map/ppermute | solution.py:361
  141.0 4.5 %collective-permute-done.55 = bf16[9,128,128]{2,1,0:T(8,128)(2,1)S(1)} collective-permute-done((bf16[9,128,128]{2,1,0:T(8,128)(2,1)S(1)}, bf16[9,128,128]{2,1,0:T(8,128)(2,1)S(1)}, u32[]{:S(2)}, u32[]{:S(2)}) %collective-permute-start.55) | collective-permute-done | bytes 294944 | tf_op jit(solution)/shard_map/ppermute | solution.py:361
  146.0 1.6 collective-permute-start.57
  149.8 4.0 %collective-permute-done.46 = bf16[9,128,128]{2,1,0:T(8,128)(2,1)S(1)} collective-permute-done((bf16[9,128,128]{2,1,0:T(8,128)(2,1)S(1)}, bf16[9,128,128]{2,1,0:T(8,128)(2,1)S(1)}, u32[]{:S(2)}, u32[]{:S(2)}) %collective-permute-start.46) | collective-permute-done | bytes 294944 | tf_op jit(solution)/shard_map/ppermute | solution.py:364
  156.8 4.6 %plan.1 = (s32[17]{0:T(128)S(1)}, s32[576]{0:T(1024)S(1)}, s32[576]{0:T(1024)S(1)}, s32[68]{0:T(128)}, s32[68]{0:T(128)}, /*index=5*/s32[36]{0:T(128)}, s32[3]{0:T(128)}) custom-call(s32[32,32]{1,0:T(8,128)} %filled.3, s32[4,32]{1,0:T(4,128)} %terms.1), custom_call_target="tpu_custom_call" | custom-call | tf_op jit(solution)/shard_map/plan/pallas_call | solution.py:179
  166.3 108.1 %conditional.1 = ((f32[1024,512]{1,0:T(8,128)}, f32[1024,512]{1,0:T(8,128)})) conditional(s32[]{:T(128)} %convert_element_type.6, (s32[17]{0:T(128)S(1)}, s32[576]{0:T(1024)S(1)}, s32[576]{0:T(1024)S(1)}, s32[68]{0:T(128)}, s32[68]{0:T(128)}, /*index=5*/s32[36]{0:T(128)}, s32[3]{0:T(128)}, bf16[4,4096,512]{2,1,0:T(8,128)(2,1)}, ...), branch_computations={%region_2.3_spmd, %region_3.4_spmd} | conditional | bytes 55052288 | solution.py:404
  166.3 108.1 %contract.2 = (f32[1024,512]{1,0:T(8,128)}, f32[1024,512]{1,0:T(8,128)}) custom-call(s32[17]{0:T(128)S(1)} %get-tuple-element.181.refs_0_, s32[576]{0:T(1024)S(1)} %get-tuple-element.182.refs_1_, s32[576]{0:T(1024)S(1)} %get-tuple-element.183.refs_2_, s32[68]{0:T(128)} %get-tuple-element.184.refs_3_, s32[68]{0:T(128)} %get-tuple-element.185.refs_4_, ...), custom_call_target="tpu_custom_call" | custom-call | tf_op jit(solution)/shard_map/cond/branch_0_fun/contract/pallas_call | solution.py:329
  275.2 3.6 %collective-permute-done.62 = f32[1024,512]{1,0:T(8,128)S(1)} collective-permute-done((f32[1024,512]{1,0:T(8,128)}, f32[1024,512]{1,0:T(8,128)S(1)}, u32[]{:S(2)}, u32[]{:S(2)}) %collective-permute-start.62) | collective-permute-done | bytes 2097184 | tf_op jit(solution)/shard_map/ppermute | solution.py:405
  279.2 3.3 %select_convert_fusion = bf16[1024,512]{1,0:T(8,128)(2,1)} fusion(f32[1024,512]{1,0:T(8,128)} %get-tuple-element.297, f32[1024,512]{1,0:T(8,128)S(1)} %collective-permute-done.62, pred[128,8,4,128]{3,2,1,0:T(4,128)(4,1)S(1)} %bitcast.6), kind=kLoop, calls=%fused_computation | loop fusion | flops 1572864 | bytes 5767168 | tf_op jit(solution)/shard_map/convert_element_type | solution.py:412
  (74 shorter events, 30.1 us)
Async XLA Ops:
  14.5 151.8 %collective-permute-start.30 = (bf16[4,1024,1024]{2,1,0:T(8,128)(2,1)}, bf16[4,1024,1024]{2,1,0:T(8,128)(2,1)}, u32[]{:S(2)}, u32[]{:S(2)}) collective-permute-start(bf16[4,1024,1024]{2,1,0:T(8,128)(2,1)} %get-tuple-element.300), channel_id=1, source_target_pairs={{0,8},{1,9},{2,10},{3,11},{4,12},{5,13},{6,14},{7,15},{8,0},{9,1},... | collective-permute-start | bytes 25165832 | tf_op jit(solution)/shard_map/ppermute | solution.py:388
  14.9 151.4 %collective-permute-start.31 = (bf16[4,1024,1024]{2,1,0:T(8,128)(2,1)}, bf16[4,1024,1024]{2,1,0:T(8,128)(2,1)}, u32[]{:S(2)}, u32[]{:S(2)}) collective-permute-start(bf16[4,1024,1024]{2,1,0:T(8,128)(2,1)} %get-tuple-element.299), channel_id=1, source_target_pairs={{0,8},{1,9},{2,10},{3,11},{4,12},{5,13},{6,14},{7,15},{8,0},{9,1},... | collective-permute-start | bytes 25165832 | tf_op jit(solution)/shard_map/ppermute | solution.py:388
  15.0 12.9 %collective-permute-start.33 = (bf16[9,128,128]{2,1,0:T(8,128)(2,1)S(1)}, bf16[9,128,128]{2,1,0:T(8,128)(2,1)S(1)}, u32[]{:S(2)}, u32[]{:S(2)}) collective-permute-start(bf16[9,128,128]{2,1,0:T(8,128)(2,1)S(1)} %get-tuple-element.293), channel_id=1, source_target_pairs={{0,2},{1,3},{2,4},{3,5},{4,6},{5,7},{6,0},{7,1},{8,10},{9,11},{10,... | collective-permute-start | bytes 884744 | tf_op jit(solution)/shard_map/ppermute | solution.py:355
  18.0 22.6 %collective-permute-start.35 = (bf16[9,128,128]{2,1,0:T(8,128)(2,1)S(1)}, bf16[9,128,128]{2,1,0:T(8,128)(2,1)S(1)}, u32[]{:S(2)}, u32[]{:S(2)}) collective-permute-start(bf16[9,128,128]{2,1,0:T(8,128)(2,1)S(1)} %get-tuple-element.293), channel_id=1, source_target_pairs={{0,4},{1,5},{2,6},{3,7},{4,0},{5,1},{6,2},{7,3},{8,12},{9,13},{10,... | collective-permute-start | bytes 884744 | tf_op jit(solution)/shard_map/ppermute | solution.py:355
  20.5 21.0 %collective-permute-start.37 = (bf16[9,128,128]{2,1,0:T(8,128)(2,1)S(1)}, bf16[9,128,128]{2,1,0:T(8,128)(2,1)S(1)}, u32[]{:S(2)}, u32[]{:S(2)}) collective-permute-start(bf16[9,128,128]{2,1,0:T(8,128)(2,1)S(1)} %get-tuple-element.293), channel_id=1, source_target_pairs={{0,6},{1,7},{2,0},{3,1},{4,2},{5,3},{6,4},{7,5},{8,14},{9,15},{10,... | collective-permute-start | bytes 884744 | tf_op jit(solution)/shard_map/ppermute | solution.py:355
  27.9 30.3 %collective-permute-start.48 = (bf16[9,128,128]{2,1,0:T(8,128)(2,1)S(1)}, bf16[9,128,128]{2,1,0:T(8,128)(2,1)S(1)}, u32[]{:S(2)}, u32[]{:S(2)}) collective-permute-start(bf16[9,128,128]{2,1,0:T(8,128)(2,1)S(1)} %get-tuple-element.294), channel_id=1, source_target_pairs={{0,2},{1,3},{2,4},{3,5},{4,6},{5,7},{6,0},{7,1},{8,10},{9,11},{10,... | collective-permute-start | bytes 884744 | tf_op jit(solution)/shard_map/ppermute | solution.py:355
  40.6 24.7 %collective-permute-start.50 = (bf16[9,128,128]{2,1,0:T(8,128)(2,1)S(1)}, bf16[9,128,128]{2,1,0:T(8,128)(2,1)S(1)}, u32[]{:S(2)}, u32[]{:S(2)}) collective-permute-start(bf16[9,128,128]{2,1,0:T(8,128)(2,1)S(1)} %get-tuple-element.294), channel_id=1, source_target_pairs={{0,4},{1,5},{2,6},{3,7},{4,0},{5,1},{6,2},{7,3},{8,12},{9,13},{10,... | collective-permute-start | bytes 884744 | tf_op jit(solution)/shard_map/ppermute | solution.py:355
  41.5 26.7 %collective-permute-start.52 = (bf16[9,128,128]{2,1,0:T(8,128)(2,1)S(1)}, bf16[9,128,128]{2,1,0:T(8,128)(2,1)S(1)}, u32[]{:S(2)}, u32[]{:S(2)}) collective-permute-start(bf16[9,128,128]{2,1,0:T(8,128)(2,1)S(1)} %get-tuple-element.294), channel_id=1, source_target_pairs={{0,6},{1,7},{2,0},{3,1},{4,2},{5,3},{6,4},{7,5},{8,14},{9,15},{10,... | collective-permute-start | bytes 884744 | tf_op jit(solution)/shard_map/ppermute | solution.py:355
  58.2 11.6 %collective-permute-start.32 = (bf16[9,128,128]{2,1,0:T(8,128)(2,1)S(1)}, bf16[9,128,128]{2,1,0:T(8,128)(2,1)S(1)}, u32[]{:S(2)}, u32[]{:S(2)}) collective-permute-start(bf16[9,128,128]{2,1,0:T(8,128)(2,1)S(1)} %get-tuple-element.293), channel_id=1, source_target_pairs={{0,1},{1,0},{2,3},{3,2},{4,5},{5,4},{6,7},{7,6},{8,9},{9,8},{10,11... | collective-permute-start | bytes 884744 | tf_op jit(solution)/shard_map/ppermute | solution.py:361
  65.3 9.9 %collective-permute-start.54 = (bf16[9,128,128]{2,1,0:T(8,128)(2,1)S(1)}, bf16[9,128,128]{2,1,0:T(8,128)(2,1)S(1)}, u32[]{:S(2)}, u32[]{:S(2)}) collective-permute-start(bf16[9,128,128]{2,1,0:T(8,128)(2,1)S(1)} %get-tuple-element.294), channel_id=1, source_target_pairs={{0,16},{1,17},{2,18},{3,19},{4,20},{5,21},{6,22},{7,23},{8,24},{9,... | collective-permute-start | bytes 884744 | tf_op jit(solution)/shard_map/ppermute | solution.py:364
  68.3 12.2 %collective-permute-start.39 = (bf16[9,128,128]{2,1,0:T(8,128)(2,1)S(1)}, bf16[9,128,128]{2,1,0:T(8,128)(2,1)S(1)}, u32[]{:S(2)}, u32[]{:S(2)}) collective-permute-start(bf16[9,128,128]{2,1,0:T(8,128)(2,1)S(1)} %get-tuple-element.293), channel_id=1, source_target_pairs={{0,16},{1,17},{2,18},{3,19},{4,20},{5,21},{6,22},{7,23},{8,24},{9,... | collective-permute-start | bytes 884744 | tf_op jit(solution)/shard_map/ppermute | solution.py:364
  69.8 12.2 %collective-permute-start.47 = (bf16[9,128,128]{2,1,0:T(8,128)(2,1)S(1)}, bf16[9,128,128]{2,1,0:T(8,128)(2,1)S(1)}, u32[]{:S(2)}, u32[]{:S(2)}) collective-permute-start(bf16[9,128,128]{2,1,0:T(8,128)(2,1)S(1)} %get-tuple-element.294), channel_id=1, source_target_pairs={{0,1},{1,0},{2,3},{3,2},{4,5},{5,4},{6,7},{7,6},{8,9},{9,8},{10,11... | collective-permute-start | bytes 884744 | tf_op jit(solution)/shard_map/ppermute | solution.py:361
  75.2 11.0 %collective-permute-start.34 = (bf16[9,128,128]{2,1,0:T(8,128)(2,1)S(1)}, bf16[9,128,128]{2,1,0:T(8,128)(2,1)}, u32[]{:S(2)}, u32[]{:S(2)}) collective-permute-start(bf16[9,128,128]{2,1,0:T(8,128)(2,1)S(1)} %collective-permute-done.33), channel_id=1, source_target_pairs={{0,1},{1,0},{2,3},{3,2},{4,5},{5,4},{6,7},{7,6},{8,9},{9,8},{10,11... | collective-permute-start | bytes 884744 | tf_op jit(solution)/shard_map/ppermute | solution.py:361
  80.4 12.0 %collective-permute-start.36 = (bf16[9,128,128]{2,1,0:T(8,128)(2,1)S(1)}, bf16[9,128,128]{2,1,0:T(8,128)(2,1)S(1)}, u32[]{:S(2)}, u32[]{:S(2)}) collective-permute-start(bf16[9,128,128]{2,1,0:T(8,128)(2,1)S(1)} %collective-permute-done.35), channel_id=1, source_target_pairs={{0,1},{1,0},{2,3},{3,2},{4,5},{5,4},{6,7},{7,6},{8,9},{9,8},{10,11... | collective-permute-start | bytes 884744 | tf_op jit(solution)/shard_map/ppermute | solution.py:361
  82.0 15.2 %collective-permute-start.38 = (bf16[9,128,128]{2,1,0:T(8,128)(2,1)S(1)}, bf16[9,128,128]{2,1,0:T(8,128)(2,1)S(1)}, u32[]{:S(2)}, u32[]{:S(2)}) collective-permute-start(bf16[9,128,128]{2,1,0:T(8,128)(2,1)S(1)} %collective-permute-done.37), channel_id=1, source_target_pairs={{0,1},{1,0},{2,3},{3,2},{4,5},{5,4},{6,7},{7,6},{8,9},{9,8},{10,11... | collective-permute-start | bytes 884744 | tf_op jit(solution)/shard_map/ppermute | solution.py:361
  86.2 11.5 %collective-permute-start.56 = (bf16[9,128,128]{2,1,0:T(8,128)(2,1)S(1)}, bf16[9,128,128]{2,1,0:T(8,128)(2,1)}, u32[]{:S(2)}, u32[]{:S(2)}) collective-permute-start(bf16[9,128,128]{2,1,0:T(8,128)(2,1)S(1)} %collective-permute-done.48), channel_id=1, source_target_pairs={{0,16},{1,17},{2,18},{3,19},{4,20},{5,21},{6,22},{7,23},{8,24},{9,... | collective-permute-start | bytes 884744 | tf_op jit(solution)/shard_map/ppermute | solution.py:364
  92.4 7.6 %collective-permute-start.58 = (bf16[9,128,128]{2,1,0:T(8,128)(2,1)S(1)}, bf16[9,128,128]{2,1,0:T(8,128)(2,1)}, u32[]{:S(2)}, u32[]{:S(2)}) collective-permute-start(bf16[9,128,128]{2,1,0:T(8,128)(2,1)S(1)} %collective-permute-done.50), channel_id=1, source_target_pairs={{0,16},{1,17},{2,18},{3,19},{4,20},{5,21},{6,22},{7,23},{8,24},{9,... | collective-permute-start | bytes 884744 | tf_op jit(solution)/shard_map/ppermute | solution.py:364
  97.2 10.1 %collective-permute-start.60 = (bf16[9,128,128]{2,1,0:T(8,128)(2,1)S(1)}, bf16[9,128,128]{2,1,0:T(8,128)(2,1)}, u32[]{:S(2)}, u32[]{:S(2)}) collective-permute-start(bf16[9,128,128]{2,1,0:T(8,128)(2,1)S(1)} %collective-permute-done.52), channel_id=1, source_target_pairs={{0,16},{1,17},{2,18},{3,19},{4,20},{5,21},{6,22},{7,23},{8,24},{9,... | collective-permute-start | bytes 884744 | tf_op jit(solution)/shard_map/ppermute | solution.py:364
  97.7 15.8 %collective-permute-start.41 = (bf16[9,128,128]{2,1,0:T(8,128)(2,1)S(1)}, bf16[9,128,128]{2,1,0:T(8,128)(2,1)S(1)}, u32[]{:S(2)}, u32[]{:S(2)}) collective-permute-start(bf16[9,128,128]{2,1,0:T(8,128)(2,1)S(1)} %collective-permute-done.33), channel_id=1, source_target_pairs={{0,16},{1,17},{2,18},{3,19},{4,20},{5,21},{6,22},{7,23},{8,24},{9,... | collective-permute-start | bytes 884744 | tf_op jit(solution)/shard_map/ppermute | solution.py:364
  100.0 19.8 %collective-permute-start.43 = (bf16[9,128,128]{2,1,0:T(8,128)(2,1)S(1)}, bf16[9,128,128]{2,1,0:T(8,128)(2,1)S(1)}, u32[]{:S(2)}, u32[]{:S(2)}) collective-permute-start(bf16[9,128,128]{2,1,0:T(8,128)(2,1)S(1)} %collective-permute-done.35), channel_id=1, source_target_pairs={{0,16},{1,17},{2,18},{3,19},{4,20},{5,21},{6,22},{7,23},{8,24},{9,... | collective-permute-start | bytes 884744 | tf_op jit(solution)/shard_map/ppermute | solution.py:364
  107.3 18.9 %collective-permute-start.45 = (bf16[9,128,128]{2,1,0:T(8,128)(2,1)S(1)}, bf16[9,128,128]{2,1,0:T(8,128)(2,1)S(1)}, u32[]{:S(2)}, u32[]{:S(2)}) collective-permute-start(bf16[9,128,128]{2,1,0:T(8,128)(2,1)S(1)} %collective-permute-done.37), channel_id=1, source_target_pairs={{0,16},{1,17},{2,18},{3,19},{4,20},{5,21},{6,22},{7,23},{8,24},{9,... | collective-permute-start | bytes 884744 | tf_op jit(solution)/shard_map/ppermute | solution.py:364
  113.5 17.3 %collective-permute-start.40 = (bf16[9,128,128]{2,1,0:T(8,128)(2,1)S(1)}, bf16[9,128,128]{2,1,0:T(8,128)(2,1)S(1)}, u32[]{:S(2)}, u32[]{:S(2)}) collective-permute-start(bf16[9,128,128]{2,1,0:T(8,128)(2,1)S(1)} %collective-permute-done.32), channel_id=1, source_target_pairs={{0,16},{1,17},{2,18},{3,19},{4,20},{5,21},{6,22},{7,23},{8,24},{9,... | collective-permute-start | bytes 884744 | tf_op jit(solution)/shard_map/ppermute | solution.py:364
  119.8 12.5 %collective-permute-start.49 = (bf16[9,128,128]{2,1,0:T(8,128)(2,1)S(1)}, bf16[9,128,128]{2,1,0:T(8,128)(2,1)S(1)}, u32[]{:S(2)}, u32[]{:S(2)}) collective-permute-start(bf16[9,128,128]{2,1,0:T(8,128)(2,1)S(1)} %collective-permute-done.48), channel_id=1, source_target_pairs={{0,1},{1,0},{2,3},{3,2},{4,5},{5,4},{6,7},{7,6},{8,9},{9,8},{10,11... | collective-permute-start | bytes 884744 | tf_op jit(solution)/shard_map/ppermute | solution.py:361
  126.1 7.6 %collective-permute-start.51 = (bf16[9,128,128]{2,1,0:T(8,128)(2,1)S(1)}, bf16[9,128,128]{2,1,0:T(8,128)(2,1)S(1)}, u32[]{:S(2)}, u32[]{:S(2)}) collective-permute-start(bf16[9,128,128]{2,1,0:T(8,128)(2,1)S(1)} %collective-permute-done.50), channel_id=1, source_target_pairs={{0,1},{1,0},{2,3},{3,2},{4,5},{5,4},{6,7},{7,6},{8,9},{9,8},{10,11... | collective-permute-start | bytes 884744 | tf_op jit(solution)/shard_map/ppermute | solution.py:361
  130.8 9.9 %collective-permute-start.53 = (bf16[9,128,128]{2,1,0:T(8,128)(2,1)S(1)}, bf16[9,128,128]{2,1,0:T(8,128)(2,1)S(1)}, u32[]{:S(2)}, u32[]{:S(2)}) collective-permute-start(bf16[9,128,128]{2,1,0:T(8,128)(2,1)S(1)} %collective-permute-done.52), channel_id=1, source_target_pairs={{0,1},{1,0},{2,3},{3,2},{4,5},{5,4},{6,7},{7,6},{8,9},{9,8},{10,11... | collective-permute-start | bytes 884744 | tf_op jit(solution)/shard_map/ppermute | solution.py:361
  132.4 13.1 %collective-permute-start.55 = (bf16[9,128,128]{2,1,0:T(8,128)(2,1)S(1)}, bf16[9,128,128]{2,1,0:T(8,128)(2,1)S(1)}, u32[]{:S(2)}, u32[]{:S(2)}) collective-permute-start(bf16[9,128,128]{2,1,0:T(8,128)(2,1)S(1)} %collective-permute-done.54), channel_id=1, source_target_pairs={{0,1},{1,0},{2,3},{3,2},{4,5},{5,4},{6,7},{7,6},{8,9},{9,8},{10,11... | collective-permute-start | bytes 884744 | tf_op jit(solution)/shard_map/ppermute | solution.py:361
  133.8 12.2 %collective-permute-start.42 = (bf16[9,128,128]{2,1,0:T(8,128)(2,1)}, bf16[9,128,128]{2,1,0:T(8,128)(2,1)S(1)}, u32[]{:S(2)}, u32[]{:S(2)}) collective-permute-start(bf16[9,128,128]{2,1,0:T(8,128)(2,1)} %collective-permute-done.34), channel_id=1, source_target_pairs={{0,16},{1,17},{2,18},{3,19},{4,20},{5,21},{6,22},{7,23},{8,24},{9,... | collective-permute-start | bytes 884744 | tf_op jit(solution)/shard_map/ppermute | solution.py:364
  140.8 7.5 %collective-permute-start.44 = (bf16[9,128,128]{2,1,0:T(8,128)(2,1)S(1)}, bf16[9,128,128]{2,1,0:T(8,128)(2,1)S(1)}, u32[]{:S(2)}, u32[]{:S(2)}) collective-permute-start(bf16[9,128,128]{2,1,0:T(8,128)(2,1)S(1)} %collective-permute-done.36), channel_id=1, source_target_pairs={{0,16},{1,17},{2,18},{3,19},{4,20},{5,21},{6,22},{7,23},{8,24},{9,... | collective-permute-start | bytes 884744 | tf_op jit(solution)/shard_map/ppermute | solution.py:364
  145.5 8.3 %collective-permute-start.46 = (bf16[9,128,128]{2,1,0:T(8,128)(2,1)S(1)}, bf16[9,128,128]{2,1,0:T(8,128)(2,1)S(1)}, u32[]{:S(2)}, u32[]{:S(2)}) collective-permute-start(bf16[9,128,128]{2,1,0:T(8,128)(2,1)S(1)} %collective-permute-done.38), channel_id=1, source_target_pairs={{0,16},{1,17},{2,18},{3,19},{4,20},{5,21},{6,22},{7,23},{8,24},{9,... | collective-permute-start | bytes 884744 | tf_op jit(solution)/shard_map/ppermute | solution.py:364
  146.0 19.4 %collective-permute-start.57 = (bf16[9,128,128]{2,1,0:T(8,128)(2,1)}, bf16[9,128,128]{2,1,0:T(8,128)(2,1)}, u32[]{:S(2)}, u32[]{:S(2)}) collective-permute-start(bf16[9,128,128]{2,1,0:T(8,128)(2,1)} %collective-permute-done.56), channel_id=1, source_target_pairs={{0,1},{1,0},{2,3},{3,2},{4,5},{5,4},{6,7},{7,6},{8,9},{9,8},{10,11... | collective-permute-start | bytes 884744 | tf_op jit(solution)/shard_map/ppermute | solution.py:361
  148.3 17.1 %collective-permute-start.59 = (bf16[9,128,128]{2,1,0:T(8,128)(2,1)}, bf16[9,128,128]{2,1,0:T(8,128)(2,1)}, u32[]{:S(2)}, u32[]{:S(2)}) collective-permute-start(bf16[9,128,128]{2,1,0:T(8,128)(2,1)} %collective-permute-done.58), channel_id=1, source_target_pairs={{0,1},{1,0},{2,3},{3,2},{4,5},{5,4},{6,7},{7,6},{8,9},{9,8},{10,11... | collective-permute-start | bytes 884744 | tf_op jit(solution)/shard_map/ppermute | solution.py:361
  154.6 11.7 %collective-permute-start.61 = (bf16[9,128,128]{2,1,0:T(8,128)(2,1)}, bf16[9,128,128]{2,1,0:T(8,128)(2,1)}, u32[]{:S(2)}, u32[]{:S(2)}) collective-permute-start(bf16[9,128,128]{2,1,0:T(8,128)(2,1)} %collective-permute-done.60), channel_id=1, source_target_pairs={{0,1},{1,0},{2,3},{3,2},{4,5},{5,4},{6,7},{7,6},{8,9},{9,8},{10,11... | collective-permute-start | bytes 884744 | tf_op jit(solution)/shard_map/ppermute | solution.py:361
  (15 other events, 464.4 us)
